TPU v7x, 32 devices: a whole 2x2x4 slice. The times are simulated.
32 devices in a mesh: row: 4 (over y, x), col: 8 (over z, core).
Axes of the slice: x: 2, y: 2, z: 4, core: 2. Of those that a mesh axis runs over, the one named last changes fastest.
Arguments:
- z_slab: float32 [1024, 1024], P('col', 'row'), may hold values from -6 to 6
- prev_factor: bfloat16 [1024, 32768], P('row', 'col'), may hold values from -0.03125 to 0.03125
- prev_solution: bfloat16 [1024, 32768], P(None, 'col'), may hold values from -6 to 6
- slab_factor: bfloat16 [1024, 1024], P('row'), may hold values from -0.09375 to 0.09375
- diag_inverse: bfloat16 [1024, 256], P('row'), may hold values from -1 to 2, as said below
Outputs:
- solved: float32 [1024, 1024], P('col', 'row')
Inputs may be any that keep to these rules, and one draw needn't show every extreme that they name: `diag_inverse`: each 256 x 256 block is lower triangular with its diagonal between 1 and 2.
All inputs are finite; a program needn't handle non-finite values.
Results may differ from a plain program's by a relative error of at most 0.0003.
Values sent between devices are 32-bit elements; how exact they have to be, the bound alone decides.
A program may use at most 64 MiB of HBM per device.

v0:
```python
import jax
import jax.numpy as jnp
from jax import lax
from jax.sharding import PartitionSpec as P


def spread(block, axis, owner):
    block = jnp.where(lax.axis_index(axis) == owner, block, jnp.zeros_like(block))
    return lax.psum(block, axis)


def precise_dot(left, right):
    return lax.dot_general(
        left,
        right,
        (((1,), (1,)), ((), ())),
        precision=lax.Precision.HIGHEST,
        preferred_element_type=jnp.float32,
    )


def on_device(z_slab, prev_factor, prev_solution, slab_factor, diag_inverse):
    row_count = z_slab.shape[0]
    block_width = diag_inverse.shape[1]
    block_rows = lax.axis_size("row")
    partial_value = lax.dot_general(
        prev_solution, prev_factor, (((1,), (1,)), ((), ())), preferred_element_type=jnp.float32
    )
    summed = lax.psum(partial_value, "col")
    fan_sum = lax.dynamic_slice_in_dim(summed, lax.axis_index("col") * row_count, row_count, 0)
    remainder = z_slab - fan_sum
    factor = slab_factor.astype(jnp.float32)
    inverse = diag_inverse.astype(jnp.float32)
    device_row = lax.axis_index("row")
    result = jnp.zeros((row_count, block_width), jnp.float32)
    updates = jnp.zeros((row_count, block_width), jnp.float32)

    def bcast_step(block_index, carry):
        result, updates = carry
        candidate = precise_dot(remainder - updates, inverse)
        arrived = spread(candidate, "row", block_index)
        result = jnp.where(device_row == block_index, arrived, result)
        columns = lax.dynamic_slice_in_dim(factor, block_index * block_width, block_width, 1)
        updates = updates + precise_dot(arrived, columns)
        return (result, updates)

    result, updates = lax.fori_loop(0, block_rows, bcast_step, (result, updates))
    return result


def solution(mesh):
    in_specs = (P("col", "row"), P("row", "col"), P(None, "col"), P("row", None), P("row", None))
    out_specs = P("col", "row")
    return jax.shard_map(
        on_device, mesh=mesh, in_specs=in_specs, out_specs=out_specs, check_vma=False
    )
```

profile of v0, /device:TPU:0, one launch (start us, length us, event | category | flops | bytes accessed | tf_op | source)
XLA Modules:
  0.0 277.1 jit_solution(165684188814202454)
XLA Ops:
  6.5 0.0 copy-start
  6.5 0.0 all-reduce.3.cloned.1.call-start
  6.5 1.6 copy-done
  8.1 6.8 %fusion.7 = f32[1024,256]{1,0:T(8,128)} fusion(bf16[1024,4096]{1,0:T(8,128)(2,1)} %param.9, bf16[256,4096]{1,0:T(8,128)(2,1)S(1)} %copy-done), kind=kOutput, calls=%fused_computation.11 | convolution fusion | flops 2147483648 | bytes 11534336 | tf_op jit(solution)/shard_map/dot_general | solution.py:26
  14.9 0.0 all-reduce.3.cloned.1.call-update
  14.9 1.1 convert_element_type.7
  16.1 0.9 convert_element_type.6
  17.0 59.6 %all-reduce.3.cloned.1.call-done = f32[1024,256]{1,0:T(8,128)} async-done(((f32[1024,256]{1,0:T(8,128)}), f32[1024,256]{1,0:T(8,128)}) %all-reduce.3.cloned.1.call-update) | async-done | bytes 1048592 | tf_op jit(solution)/shard_map/psum | solution.py:29
  76.6 1.6 dynamic-slice_subtract_fusion
  78.3 192.3 %while.16 = (s32[]{:T(128)}, f32[128,256]{1,0:T(8,128)}, f32[128,256]{1,0:T(8,128)S(1)}, s32[]{:T(128)}, f32[128,256]{1,0:T(8,128)}, /*index=5*/f32[256,256]{1,0...) while((s32[]{:T(128)}, f32[128,256]{1,0:T(8,128)}, ...), condition=%wide.region_3.4_spmd.clone, body=%wide.region_1.3_spmd.clone.sunk | while | flops 201588736 | bytes 2490639 | solution.py:47
  78.3 0.0 all-reduce.5.cloned.1.call-start
  78.3 1.9 convolution_select_fusion.2
  80.2 0.0 all-reduce.5.cloned.1.call-update
  80.3 42.7 %all-reduce.5.cloned.1.call-done = f32[128,256]{1,0:T(8,128)} async-done(((f32[128,256]{1,0:T(8,128)}), f32[128,256]{1,0:T(8,128)}) %all-reduce.5.cloned.1.call-update) | async-done | bytes 131088 | tf_op jit(solution)/shard_map/while/body/eval_jaxpr/psum | solution.py:9
  123.0 1.4 convolution_add_fusion.2
  124.3 1.6 select_select_fusion.2
  125.9 2.0 convolution_select_fusion.2
  127.9 0.0 all-reduce.5.cloned.1.call-update
  127.9 42.9 %all-reduce.5.cloned.1.call-done = f32[128,256]{1,0:T(8,128)} async-done(((f32[128,256]{1,0:T(8,128)}), f32[128,256]{1,0:T(8,128)}) %all-reduce.5.cloned.1.call-update) | async-done | bytes 131088 | tf_op jit(solution)/shard_map/while/body/eval_jaxpr/psum | solution.py:9
  170.8 1.4 convolution_add_fusion.2
  172.1 1.6 select_select_fusion.2
  173.7 0.0 all-reduce.5.cloned.1.call-start
  173.7 1.9 convolution_select_fusion.2
  175.7 0.0 all-reduce.5.cloned.1.call-update
  175.7 43.5 %all-reduce.5.cloned.1.call-done = f32[128,256]{1,0:T(8,128)} async-done(((f32[128,256]{1,0:T(8,128)}), f32[128,256]{1,0:T(8,128)}) %all-reduce.5.cloned.1.call-update) | async-done | bytes 131088 | tf_op jit(solution)/shard_map/while/body/eval_jaxpr/psum | solution.py:9
  219.2 1.4 convolution_add_fusion.2
  220.6 1.6 select_select_fusion.2
  222.2 1.9 convolution_select_fusion.2
  224.1 0.0 all-reduce.5.cloned.1.call-update
  224.2 43.4 %all-reduce.5.cloned.1.call-done = f32[128,256]{1,0:T(8,128)} async-done(((f32[128,256]{1,0:T(8,128)}), f32[128,256]{1,0:T(8,128)}) %all-reduce.5.cloned.1.call-update) | async-done | bytes 131088 | tf_op jit(solution)/shard_map/while/body/eval_jaxpr/psum | solution.py:9
  267.6 1.4 convolution_add_fusion.2
  269.0 1.6 select_select_fusion.2
  (4 shorter events, 0.0 us)
Async XLA Ops:
  6.5 1.6 copy-start
  6.5 70.1 %all-reduce.3.cloned.1.call-start = ((), (), s32[]{:S(2)}) async-start(), calls=%async_computation | async-start | bytes 2097152 | tf_op jit(solution)/shard_map/psum | solution.py:29
  78.3 44.7 %all-reduce.5.cloned.1.call-start = ((), (), s32[]{:S(2)}) async-start(), calls=%async_computation.1 | async-start | bytes 262144 | tf_op jit(solution)/shard_map/while/body/eval_jaxpr/psum | solution.py:9
  125.9 44.9 %all-reduce.5.cloned.1.call-start = ((), (), s32[]{:S(2)}) async-start(), calls=%async_computation.1 | async-start | bytes 262144 | tf_op jit(solution)/shard_map/while/body/eval_jaxpr/psum | solution.py:9
  173.7 45.5 %all-reduce.5.cloned.1.call-start = ((), (), s32[]{:S(2)}) async-start(), calls=%async_computation.1 | async-start | bytes 262144 | tf_op jit(solution)/shard_map/while/body/eval_jaxpr/psum | solution.py:9
  222.2 45.4 %all-reduce.5.cloned.1.call-start = ((), (), s32[]{:S(2)}) async-start(), calls=%async_computation.1 | async-start | bytes 262144 | tf_op jit(solution)/shard_map/while/body/eval_jaxpr/psum | solution.py:9
Sparse Core Ops, SparseCore 0:
  15.0 61.5 all-reduce.2
  82.0 40.9 all-reduce.4
  129.6 41.1 all-reduce.4
  177.1 42.0 all-reduce.4
  225.6 41.9 all-reduce.4
where the time goes:
time: 278 us; the launch traced here: 277 us
  waiting for transfers between devices  232 us (83%)
  matrix products  20 us (7%)
  between operations  13.1 us (5%)
  other arithmetic  10.1 us (4%)
    psum x4, waiting for transfers between devices, spread(): return lax.psum(block, axis)  173 us
    psum x1, waiting for transfers between devices, on_device(): summed = lax.psum(partial_value, 'col')  59.6 us
    dot_general x8, matrix products, precise_dot(): lax.dot_general(left, right, (((1,), (1,)), ((), ())), precision=lax.Prec...  13.2 us
    dot_general x1, matrix products, on_device(): lax.dot_general(prev_solution, prev_factor, (((1,), (1,)), ((), ())), pre...  6.76 us
    select_n x4, other arithmetic, bcast_step(): result = jnp.where(device_row == block_index, arrived, result)  6.36 us
  transfers between devices with their start and end apart: 5, of which 5 were waited for; matrix products, arithmetic and copies ran while one was open for 1% of the time, Pallas kernels for 0%

commit v1 on v0

--- a/solution.py
+++ b/solution.py
@@ -6,7 +6,7 @@
 
 def spread(block, axis, owner):
     block = jnp.where(lax.axis_index(axis) == owner, block, jnp.zeros_like(block))
-    return lax.psum(block, axis)
+    return jnp.sum(lax.all_gather(block, axis), axis=0)
 
 
 def precise_dot(left, right):

time: 278 us -> 133 us (0.48)
  waiting for transfers between devices: 232 us -> 60.6 us
  blocking collectives: 0 us -> 39.7 us
  other arithmetic: 10.1 us -> 2.31 us
  matrix products: 20 us -> 14 us
    psum x4 -> x0, waiting for transfers between devices: 173 us -> none  [spread(): return lax.psum(block, axis)]
    all_gather x0 -> x4, blocking collectives: none -> 39.7 us  [spread(): return jnp.sum(lax.all_gather(block, axis), axis=0)]
    select_n x4, other arithmetic: 6.36 us -> 0.14 us  [bcast_step(): result = jnp.where(device_row == block_index, arrived, result)]
    dot_general x8, matrix products: 13.2 us -> 7.24 us  [precise_dot(): lax.dot_general(left, right, (((1,), (1,)), ((), ())), precision=lax.Prec...]
  transfers between devices with their start and end apart: 5 -> 1, of which waited for: 5 -> 1; matrix products, arithmetic and copies ran while one was open for 1% -> 1% of each run, Pallas kernels for 0% -> 0%
where the time goes in v1:
time: 133 us
  waiting for transfers between devices  60.6 us (46%)
  blocking collectives  39.7 us (30%)
  matrix products  14 us (11%)
  between operations  13.5 us (10%)
  other arithmetic  2.31 us (2%)
  local copies, waits for them, and re-layouts  2.2 us (2%)
    psum x1, waiting for transfers between devices, on_device(): summed = lax.psum(partial_value, 'col')  60.6 us
    all_gather x4, blocking collectives, spread(): return jnp.sum(lax.all_gather(block, axis), axis=0)  39.7 us
    dot_general x8, matrix products, precise_dot(): lax.dot_general(left, right, (((1,), (1,)), ((), ())), precision=lax.Prec...  7.24 us
    dot_general x1, matrix products, on_device(): lax.dot_general(prev_solution, prev_factor, (((1,), (1,)), ((), ())), pre...  6.74 us
  transfers between devices with their start and end apart: 1, of which 1 were waited for; matrix products, arithmetic and copies ran while one was open for 1% of the time, Pallas kernels for 0%

profile of v1, /device:TPU:0, one launch (start us, length us, event | category | flops | bytes accessed | tf_op | source)
XLA Modules:
  0.0 132.5 jit_solution(3107362448296787316)
XLA Ops:
  6.5 0.0 copy-start
  6.5 0.0 copy-start.2
  6.5 0.0 copy-start.3
  6.5 0.0 copy-start.4
  6.5 0.0 all-reduce.2.cloned.1.call-start
  6.6 1.5 %copy-done = bf16[256,4096]{1,0:T(8,128)(2,1)S(1)} copy-done((bf16[256,4096]{1,0:T(8,128)(2,1)S(1)}, bf16[256,4096]{1,0:T(8,128)(2,1)}, u32[]{:S(2)}) %copy-start) | copy-done | bytes 2097176
  8.1 6.7 %fusion.7 = f32[1024,256]{1,0:T(8,128)} fusion(bf16[1024,4096]{1,0:T(8,128)(2,1)} %param.9, bf16[256,4096]{1,0:T(8,128)(2,1)S(1)} %copy-done), kind=kOutput, calls=%fused_computation.11 | convolution fusion | flops 2147483648 | bytes 11534336 | tf_op jit(solution)/shard_map/dot_general | solution.py:26
  14.9 0.0 all-reduce.2.cloned.1.call-update
  14.9 0.0 copy-done.2
  14.9 1.1 convert_element_type.7
  16.0 0.0 copy-done.3
  16.0 60.6 %all-reduce.2.cloned.1.call-done = f32[1024,256]{1,0:T(8,128)} async-done(((f32[1024,256]{1,0:T(8,128)}), f32[1024,256]{1,0:T(8,128)}) %all-reduce.2.cloned.1.call-update) | async-done | bytes 1048592 | tf_op jit(solution)/shard_map/psum | solution.py:29
  76.6 0.0 copy-done.4
  76.6 0.9 dynamic-slice_subtract_fusion
  77.5 47.5 %while.16 = (s32[]{:T(128)}, f32[128,256]{1,0:T(8,128)S(1)}, f32[128,256]{1,0:T(8,128)S(1)}, s32[]{:T(128)}, f32[128,256]{1,0:T(8,128)S(1)}, /*index=5*/f32[256,...) while((s32[]{:T(128)}, f32[128,256]{1,0:T(8,128)S(1)}, ...), condition=%wide.region_3.4_spmd.clone, body=%wide.region_1.3_spmd.clone.sunk | while | flops 201654272 | bytes 3014899 | solution.py:47
  77.6 0.4 convolution_select_fusion.2
  78.0 10.7 %all-gather.3 = f32[512,256]{1,0:T(8,128)S(1)} all-gather(f32[128,256]{1,0:T(8,128)S(1)} %convolution_select_fusion.2), channel_id=2, replica_groups=mesh['row'=4,'col'=8] {'row'}, dimensions={0}, use_global_device_ids=true | all-gather | bytes 655360 | tf_op jit(solution)/shard_map/while/body/eval_jaxpr/all_gather | solution.py:9
  88.7 1.4 %convolution_add_fusion.2 = f32[128,256]{1,0:T(8,128)S(1)} fusion(f32[128,256]{1,0:T(8,128)S(1)} %reduce_sum.15, f32[256,1024]{1,0:T(8,128)} %get-tuple-element.243, s32[]{:T(128)S(6)} %select_n.59, f32[128,256]{1,0:T(8,128)S(1)} %get-tuple-element.226, pred[]{:T(512)S(6)} %compare.3), kind=kOutput, calls=%fused_computation.clone.1 | convolution fusion | flops 100728832 | bytes 655365 | tf_op jit(solution)/shard_map/while/body/eval_jaxpr/dot_general | solution.py:13
  90.2 0.4 convolution_select_fusion.2
  90.6 9.7 %all-gather.3 = f32[512,256]{1,0:T(8,128)S(1)} all-gather(f32[128,256]{1,0:T(8,128)S(1)} %convolution_select_fusion.2), channel_id=2, replica_groups=mesh['row'=4,'col'=8] {'row'}, dimensions={0}, use_global_device_ids=true | all-gather | bytes 655360 | tf_op jit(solution)/shard_map/while/body/eval_jaxpr/all_gather | solution.py:9
  100.3 1.4 %convolution_add_fusion.2 = f32[128,256]{1,0:T(8,128)S(1)} fusion(f32[128,256]{1,0:T(8,128)S(1)} %reduce_sum.15, f32[256,1024]{1,0:T(8,128)} %get-tuple-element.243, s32[]{:T(128)S(6)} %select_n.59, f32[128,256]{1,0:T(8,128)S(1)} %get-tuple-element.226, pred[]{:T(512)S(6)} %compare.3), kind=kOutput, calls=%fused_computation.clone.1 | convolution fusion | flops 100728832 | bytes 655365 | tf_op jit(solution)/shard_map/while/body/eval_jaxpr/dot_general | solution.py:13
  101.8 0.4 convolution_select_fusion.2
  102.2 9.6 %all-gather.3 = f32[512,256]{1,0:T(8,128)S(1)} all-gather(f32[128,256]{1,0:T(8,128)S(1)} %convolution_select_fusion.2), channel_id=2, replica_groups=mesh['row'=4,'col'=8] {'row'}, dimensions={0}, use_global_device_ids=true | all-gather | bytes 655360 | tf_op jit(solution)/shard_map/while/body/eval_jaxpr/all_gather | solution.py:9
  111.8 1.4 %convolution_add_fusion.2 = f32[128,256]{1,0:T(8,128)S(1)} fusion(f32[128,256]{1,0:T(8,128)S(1)} %reduce_sum.15, f32[256,1024]{1,0:T(8,128)} %get-tuple-element.243, s32[]{:T(128)S(6)} %select_n.59, f32[128,256]{1,0:T(8,128)S(1)} %get-tuple-element.226, pred[]{:T(512)S(6)} %compare.3), kind=kOutput, calls=%fused_computation.clone.1 | convolution fusion | flops 100728832 | bytes 655365 | tf_op jit(solution)/shard_map/while/body/eval_jaxpr/dot_general | solution.py:13
  113.3 0.4 convolution_select_fusion.2
  113.7 9.7 %all-gather.3 = f32[512,256]{1,0:T(8,128)S(1)} all-gather(f32[128,256]{1,0:T(8,128)S(1)} %convolution_select_fusion.2), channel_id=2, replica_groups=mesh['row'=4,'col'=8] {'row'}, dimensions={0}, use_global_device_ids=true | all-gather | bytes 655360 | tf_op jit(solution)/shard_map/while/body/eval_jaxpr/all_gather | solution.py:9
  123.5 1.4 %convolution_add_fusion.2 = f32[128,256]{1,0:T(8,128)S(1)} fusion(f32[128,256]{1,0:T(8,128)S(1)} %reduce_sum.15, f32[256,1024]{1,0:T(8,128)} %get-tuple-element.243, s32[]{:T(128)S(6)} %select_n.59, f32[128,256]{1,0:T(8,128)S(1)} %get-tuple-element.226, pred[]{:T(512)S(6)} %compare.3), kind=kOutput, calls=%fused_computation.clone.1 | convolution fusion | flops 100728832 | bytes 655365 | tf_op jit(solution)/shard_map/while/body/eval_jaxpr/dot_general | solution.py:13
  125.0 0.0 copy-start.1
  125.0 0.6 copy-done.1
  (11 shorter events, 0.3 us)
Async XLA Ops:
  6.5 1.6 %copy-start = (bf16[256,4096]{1,0:T(8,128)(2,1)S(1)}, bf16[256,4096]{1,0:T(8,128)(2,1)}, u32[]{:S(2)}) copy-start(bf16[256,4096]{1,0:T(8,128)(2,1)} %param.8) | copy-start | bytes 6291460
  6.5 8.4 %copy-start.2 = (bf16[256,1024]{1,0:T(8,128)(2,1)S(1)}, bf16[256,1024]{1,0:T(8,128)(2,1)}, u32[]{:S(2)}) copy-start(bf16[256,1024]{1,0:T(8,128)(2,1)} %param.10) | copy-start | bytes 1572868
  6.5 9.5 %copy-start.3 = (bf16[256,256]{1,0:T(8,128)(2,1)S(1)}, bf16[256,256]{1,0:T(8,128)(2,1)}, u32[]{:S(2)}) copy-start(bf16[256,256]{1,0:T(8,128)(2,1)} %param.11) | copy-start | bytes 393220
  6.5 70.1 %copy-start.4 = (f32[128,256]{1,0:T(8,128)S(1)}, f32[128,256]{1,0:T(8,128)}, u32[]{:S(2)}) copy-start(f32[128,256]{1,0:T(8,128)} %param.7) | copy-start | bytes 393220
  6.5 70.1 %all-reduce.2.cloned.1.call-start = ((), (), s32[]{:S(2)}) async-start(), calls=%async_computation | async-start | bytes 2097152 | tf_op jit(solution)/shard_map/psum | solution.py:29
  125.0 0.7 copy-start.1
Sparse Core Ops, SparseCore 0:
  15.0 61.5 all-reduce.1
